TPU v7x, 256 devices: a whole 4x4x8 slice. The times are simulated.
256 devices in a mesh: tm: 32 (over x, y, core), space: 8 (over z).
Axes of the slice: x: 4, y: 4, z: 8, core: 2. Of those that a mesh axis runs over, the one named last changes fastest.
Arguments:
- sep_block: float32 [32, 1536, 1536], P('tm', 'space'), may hold values from -1 to 10, as said below
- own_couple: bfloat16 [32, 1536, 1536], P('tm', 'space'), may hold values from -0.1875 to 0.1875
- prev_couple: bfloat16 [32, 1536, 1536], P('tm', 'space'), may hold values from -0.1875 to 0.1875
- inner_diag: float32 [32, 1536], P('tm'), may hold values from 0.5 to 4
Outputs:
- reduced_blocks: float32 [32, 1536, 1536], P('tm', 'space')
- left_links: bfloat16 [32, 1536, 1536], P('tm', 'space')
Inputs may be any that keep to these rules, and one draw needn't show every extreme that they name: sep_block is symmetric in its last two dimensions; its diagonal entries lie between 3.5 and 10.
All inputs are finite; a program needn't handle non-finite values.
Results may differ from a plain program's by a relative error of at most 0.0083.
Values may be sent and summed in bfloat16 or wider, within the bound.
A program may use at most 64 MiB of HBM per device.

v0:
```python
import jax
import jax.numpy as jnp
from jax import lax
from jax.sharding import PartitionSpec as P


def passed_along(block, axis, distance):
    devices = range(lax.axis_size(axis))
    route = [(i - distance, i) for i in devices if i - distance in devices]
    return lax.ppermute(block, axis, route)


def scaled_by(matrix, factors):
    return (matrix.astype(jnp.float32) * factors.astype(jnp.float32)[None, :]).astype(jnp.bfloat16)


def outer_form(left_side, right_side):
    return jnp.einsum("ik,jk->ij", left_side, right_side, preferred_element_type=jnp.float32)


def reduce_level(schur, link, distance, partition, row_start):
    row_count = schur.shape[0]
    diag_block = lax.dynamic_slice_in_dim(schur, row_start, row_count, 1)
    scale_local = (1.0 / jnp.maximum(jnp.diagonal(diag_block), 1.0)).astype(jnp.bfloat16)
    scale_full = lax.all_gather(scale_local, "space", axis=0, tiled=True)
    own_full = lax.all_gather(link, "space", axis=0, tiled=True)
    next_full, next_scale = passed_along((own_full, scale_full), "tm", -distance)
    flipped = lax.dynamic_slice_in_dim(next_full, row_start, row_count, 1).T
    flipped_scaled = scaled_by(flipped, scale_full)
    right_form = jnp.dot(flipped_scaled, next_full, preferred_element_type=jnp.float32)
    own_scaled = scaled_by(link, scale_full)
    fill_link = (-jnp.dot(own_scaled, next_full, preferred_element_type=jnp.float32)).astype(
        jnp.bfloat16
    )
    right_recv, fill_recv = (
        passed_along(right_form.astype(jnp.bfloat16), "tm", distance).astype(right_form.dtype),
        passed_along(fill_link.astype(jnp.float32).astype(jnp.bfloat16), "tm", distance).astype(
            jnp.float32
        ),
    )
    next_local = lax.dynamic_slice_in_dim(next_full, row_start, row_count, 0)
    next_scaled = scaled_by(next_local, next_scale)
    left_form = outer_form(next_scaled, next_full)
    new_schur = schur - left_form - right_recv
    receiver = partition % (2 * distance) == 2 * distance - 1
    return (
        jnp.where(receiver, new_schur, schur),
        jnp.where(receiver, fill_recv.astype(jnp.bfloat16), link),
    )


def on_device(sep_block, own_couple, prev_couple, inner_diag):
    separator = sep_block[0]
    own_rows = own_couple[0]
    prev_rows = prev_couple[0]
    reciprocal = 1.0 / inner_diag[0]
    row_count = separator.shape[0]
    row_start = lax.axis_index("space") * row_count
    partition = lax.axis_index("tm")
    own_scaled = scaled_by(own_rows, reciprocal)
    prev_scaled = scaled_by(prev_rows, reciprocal)
    couple_pair = jnp.stack([own_rows, prev_rows])
    piece_rows = lax.all_gather(couple_pair, "space", axis=1, tiled=True)
    local_forms = jnp.stack(
        [
            outer_form(own_scaled, piece_rows[0]),
            outer_form(prev_scaled, piece_rows[1]),
            outer_form(prev_scaled, piece_rows[0]),
        ]
    )
    incoming = passed_along(local_forms[1], "tm", -1)
    schur = separator - local_forms[0] - incoming
    link = (-local_forms[2]).astype(jnp.bfloat16)
    link = jnp.where(partition == 0, jnp.zeros_like(link), link)
    for distance in (1, 2):
        schur, link = reduce_level(schur, link, distance, partition, row_start)
    return (schur[None], link[None])


def solution(mesh):
    placed = (P("tm", "space", None), P("tm", "space", None), P("tm", "space", None), P("tm", None))
    return jax.shard_map(
        on_device,
        mesh=mesh,
        in_specs=placed,
        out_specs=(P("tm", "space", None), P("tm", "space", None)),
        check_vma=False,
    )
```

profile of v0, /device:TPU:6, one launch (start us, length us, event | category | flops | bytes accessed | tf_op | source)
XLA Modules:
  0.0 520.2 jit_solution(10280945665940516997)
XLA Ops:
  10.3 107.0 %all-gather.4.cloned.1.call-done = bf16[2,1536,1536]{2,1,0:T(8,128)(2,1)} async-done(((bf16[2,192,1536]{2,1,0:T(8,128)(2,1)}), bf16[2,1536,1536]{2,1,0:T(8,128)(2,1)}) %all-gather.4.cloned.1.call-update) | async-done | bytes 9437200 | tf_op jit(solution)/shard_map/all_gather | solution.py:63
  117.3 4.8 fusion.14
  122.2 58.4 %all-gather.6.cloned.1.call-done = bf16[1536,1536]{1,0:T(8,128)(2,1)} async-done(((bf16[192,1536]{1,0:T(8,128)(2,1)}), bf16[1536,1536]{1,0:T(8,128)(2,1)}) %all-gather.6.cloned.1.call-update) | async-done | bytes 4718608 | tf_op jit(solution)/shard_map/all_gather | solution.py:26
  180.6 4.4 collective-permute-start.1
  185.0 5.0 fusion
  190.1 2.6 collective-permute-start
  193.8 55.8 %collective-permute-done = f32[192,1536]{1,0:T(8,128)} collective-permute-done((f32[192,1536]{1,0:T(8,128)}, f32[192,1536]{1,0:T(8,128)}, u32[]{:S(2)}, u32[]{:S(2)}) %collective-permute-start) | collective-permute-done | bytes 1179680 | tf_op jit(solution)/shard_map/ppermute | solution.py:10
  249.6 4.4 fusion.4
  256.4 15.5 %all-reduce = bf16[1536]{0:T(1024)(128)(2,1)S(1)} all-reduce(bf16[1536]{0:T(1024)(128)(2,1)S(1)} %dynamic-update-slice), channel_id=1, replica_groups=mesh['tm'=32,'space'=8] {'space'}, use_global_device_ids=true, to_apply=%add | all-reduce | flops 1536 | bytes 6144
  271.9 3.4 fusion.12
  277.3 11.4 %collective-permute-done.4 = bf16[192,1536]{1,0:T(8,128)(2,1)S(1)} collective-permute-done((bf16[192,1536]{1,0:T(8,128)(2,1)S(1)}, bf16[192,1536]{1,0:T(8,128)(2,1)S(1)}, u32[]{:S(2)}, u32[]{:S(2)}) %collective-permute-start.4) | collective-permute-done | bytes 589856 | tf_op jit(solution)/shard_map/ppermute | solution.py:10
  289.5 57.0 %all-gather.8.cloned.1.call-done = bf16[1536,1536]{1,0:T(8,128)(2,1)} async-done(((bf16[192,1536]{1,0:T(8,128)(2,1)}), bf16[1536,1536]{1,0:T(8,128)(2,1)}) %all-gather.8.cloned.1.call-update) | async-done | bytes 4718608 | tf_op jit(solution)/shard_map/all_gather | solution.py:26
  346.6 4.9 collective-permute-start.5
  351.5 4.0 convolution_convert_fusion.1
  357.4 5.8 %collective-permute-start.2 = (bf16[1536]{0:T(1024)(128)(2,1)S(1)}, bf16[1536]{0:T(1024)(128)(2,1)S(1)}, u32[]{:S(2)}, u32[]{:S(2)}) collective-permute-start(bf16[1536]{0:T(1024)(128)(2,1)S(1)} %all-reduce), channel_id=1, source_target_pairs={{8,0},{16,8},{24,16},{32,24},{40,32},{48,40},{56,48},{64,56},{72,6... | collective-permute-start | bytes 9224 | tf_op jit(solution)/shard_map/ppermute | solution.py:10
  363.1 89.7 %collective-permute-done.2 = bf16[1536]{0:T(1024)(128)(2,1)S(1)} collective-permute-done((bf16[1536]{0:T(1024)(128)(2,1)S(1)}, bf16[1536]{0:T(1024)(128)(2,1)S(1)}, u32[]{:S(2)}, u32[]{:S(2)}) %collective-permute-start.2) | collective-permute-done | bytes 3104 | tf_op jit(solution)/shard_map/ppermute | solution.py:10
  452.9 4.2 fusion.9
  459.4 15.5 %all-reduce.1 = bf16[1536]{0:T(1024)(128)(2,1)S(1)} all-reduce(bf16[1536]{0:T(1024)(128)(2,1)S(1)} %dynamic-update-slice.1), channel_id=1, replica_groups=mesh['tm'=32,'space'=8] {'space'}, use_global_device_ids=true, to_apply=%add.1 | all-reduce | flops 1536 | bytes 6144
  475.0 4.3 fusion.13
  481.1 3.9 convolution_convert_fusion
  487.5 5.6 %collective-permute-start.6 = (bf16[1536]{0:T(1024)(128)(2,1)S(1)}, bf16[1536]{0:T(1024)(128)(2,1)S(1)}, u32[]{:S(2)}, u32[]{:S(2)}) collective-permute-start(bf16[1536]{0:T(1024)(128)(2,1)S(1)} %all-reduce.1), channel_id=1, source_target_pairs={{16,0},{24,8},{32,16},{40,24},{48,32},{56,40},{64,48},{72,56},{80,... | collective-permute-start | bytes 9224 | tf_op jit(solution)/shard_map/ppermute | solution.py:10
  494.4 5.3 %collective-permute-done.8 = bf16[192,1536]{1,0:T(8,128)(2,1)S(1)} collective-permute-done((bf16[192,1536]{1,0:T(8,128)(2,1)}, bf16[192,1536]{1,0:T(8,128)(2,1)S(1)}, u32[]{:S(2)}, u32[]{:S(2)}) %collective-permute-start.8) | collective-permute-done | bytes 589856 | tf_op jit(solution)/shard_map/ppermute | solution.py:10
  500.6 7.8 %collective-permute-done.7 = bf16[192,1536]{1,0:T(8,128)(2,1)S(1)} collective-permute-done((bf16[192,1536]{1,0:T(8,128)(2,1)S(1)}, bf16[192,1536]{1,0:T(8,128)(2,1)S(1)}, u32[]{:S(2)}, u32[]{:S(2)}) %collective-permute-start.7) | collective-permute-done | bytes 589856 | tf_op jit(solution)/shard_map/ppermute | solution.py:10
  508.4 5.2 %fusion.7 = f32[1,192,1536]{2,1,0:T(8,128)} fusion(f32[192,1536]{1,0:T(8,128)S(1)} %fusion.9, bf16[1536,1536]{1,0:T(8,128)(2,1)} %collective-permute-done.5, bf16[192,1536]{1,0:T(8,128)(2,1)S(1)} %collective-permute-done.7, f32[1536]{0:T(1024)S(1)} %convert_element_type.132, s32[]{:T(128)S(6)} %select_n.61, pred[]{:T(512)S(6)} %eq.12), kind=kOutput, calls=%fused_computation.14 | convolution fusion | flops 908034048 | bytes 8263685 | tf_op jit(solution)/shard_map/ik,jk->ij/dot_general | solution.py:18
  (48 shorter events, 19.6 us)
Async XLA Ops:
  7.2 110.1 %all-gather.4.cloned.1.call-start = ((), (), s32[]{:S(2)}) async-start(), calls=%async_computation | async-start | bytes 10616832 | tf_op jit(solution)/shard_map/all_gather | solution.py:63
  9.6 0.7 copy-start.5
  9.6 107.7 %copy-start.4 = (bf16[1,192,1536]{2,1,0:T(8,128)(2,1)S(1)}, bf16[1,192,1536]{2,1,0:T(8,128)(2,1)}, u32[]{:S(2)}) copy-start(bf16[1,192,1536]{2,1,0:T(8,128)(2,1)} %param.6) | copy-start | bytes 1769476
  9.6 171.0 %all-gather.6.cloned.1.call-start = ((), (), s32[]{:S(2)}) async-start(), calls=%async_computation.1 | async-start | bytes 5308416 | tf_op jit(solution)/shard_map/all_gather | solution.py:26
  122.1 70.5 %copy-start.6 = (u32[256]{0:T(256)S(1)}, u32[256]{0:T(256)}, u32[]{:S(2)}) copy-start(u32[256]{0:T(256)} %constant.83) | copy-start | bytes 3076
  122.2 127.4 %copy-start.1 = (bf16[1,192,1536]{2,1,0:T(8,128)(2,1)S(1)}, bf16[1,192,1536]{2,1,0:T(8,128)(2,1)}, u32[]{:S(2)}) copy-start(bf16[1,192,1536]{2,1,0:T(8,128)(2,1)} %param.5) | copy-start | bytes 1769476
  122.2 127.4 %copy-start.3 = (f32[1,192,1536]{2,1,0:T(8,128)S(1)}, f32[1,192,1536]{2,1,0:T(8,128)}, u32[]{:S(2)}) copy-start(f32[1,192,1536]{2,1,0:T(8,128)} %param.4) | copy-start | bytes 3538948
  122.2 224.4 %all-gather.8.cloned.1.call-start = ((), (), s32[]{:S(2)}) async-start(), calls=%async_computation.2 | async-start | bytes 5308416 | tf_op jit(solution)/shard_map/all_gather | solution.py:26
  180.6 91.2 %collective-permute-start.1 = (bf16[1536,1536]{1,0:T(8,128)(2,1)}, bf16[1536,1536]{1,0:T(8,128)(2,1)}, u32[]{:S(2)}, u32[]{:S(2)}) collective-permute-start(bf16[1536,1536]{1,0:T(8,128)(2,1)} %all-gather.6.cloned.1.call-done), channel_id=1, source_target_pairs={{8,0},{16,8},{24,16},{32,24},{40,32},{48,40},{56,48},{64,56},{72,6... | collective-permute-start | bytes 14155784 | tf_op jit(solution)/shard_map/ppermute | solution.py:10
  190.1 59.5 %collective-permute-start = (f32[192,1536]{1,0:T(8,128)}, f32[192,1536]{1,0:T(8,128)}, u32[]{:S(2)}, u32[]{:S(2)}) collective-permute-start(f32[192,1536]{1,0:T(8,128)} %fusion), channel_id=1, source_target_pairs={{8,0},{16,8},{24,16},{32,24},{40,32},{48,40},{56,48},{64,56},{72,6... | collective-permute-start | bytes 3538952 | tf_op jit(solution)/shard_map/ppermute | solution.py:10
  254.0 17.8 %copy-start.2 = (bf16[192,1536]{1,0:T(8,128)(2,1)S(1)}, bf16[192,1536]{1,0:T(8,128)(2,1)}, u32[]{:S(2)}) copy-start(bf16[192,1536]{1,0:T(8,128)(2,1)} %fusion.14) | copy-start | bytes 1769476
  275.3 13.3 %collective-permute-start.4 = (bf16[192,1536]{1,0:T(8,128)(2,1)S(1)}, bf16[192,1536]{1,0:T(8,128)(2,1)S(1)}, u32[]{:S(2)}, u32[]{:S(2)}) collective-permute-start(bf16[192,1536]{1,0:T(8,128)(2,1)S(1)} %fusion.12), channel_id=1, source_target_pairs={{0,8},{8,16},{16,24},{24,32},{32,40},{40,48},{48,56},{56,64},{64,7... | collective-permute-start | bytes 1769480 | tf_op jit(solution)/shard_map/ppermute | solution.py:10
  346.6 128.4 %collective-permute-start.5 = (bf16[1536,1536]{1,0:T(8,128)(2,1)}, bf16[1536,1536]{1,0:T(8,128)(2,1)}, u32[]{:S(2)}, u32[]{:S(2)}) collective-permute-start(bf16[1536,1536]{1,0:T(8,128)(2,1)} %all-gather.8.cloned.1.call-done), channel_id=1, source_target_pairs={{16,0},{24,8},{32,16},{40,24},{48,32},{56,40},{64,48},{72,56},{80,... | collective-permute-start | bytes 14155784 | tf_op jit(solution)/shard_map/ppermute | solution.py:10
  355.4 97.4 %collective-permute-start.3 = (bf16[192,1536]{1,0:T(8,128)(2,1)S(1)}, bf16[192,1536]{1,0:T(8,128)(2,1)S(1)}, u32[]{:S(2)}, u32[]{:S(2)}) collective-permute-start(bf16[192,1536]{1,0:T(8,128)(2,1)S(1)} %convolution_convert_fusion.1), channel_id=1, source_target_pairs={{0,8},{8,16},{16,24},{24,32},{32,40},{40,48},{48,56},{56,64},{64,7... | collective-permute-start | bytes 1769480 | tf_op jit(solution)/shard_map/ppermute | solution.py:10
  357.4 95.5 %collective-permute-start.2 = (bf16[1536]{0:T(1024)(128)(2,1)S(1)}, bf16[1536]{0:T(1024)(128)(2,1)S(1)}, u32[]{:S(2)}, u32[]{:S(2)}) collective-permute-start(bf16[1536]{0:T(1024)(128)(2,1)S(1)} %all-reduce), channel_id=1, source_target_pairs={{8,0},{16,8},{24,16},{32,24},{40,32},{48,40},{56,48},{64,56},{72,6... | collective-permute-start | bytes 9224 | tf_op jit(solution)/shard_map/ppermute | solution.py:10
  457.1 17.9 %copy-start = (bf16[192,1536]{1,0:T(8,128)(2,1)S(1)}, bf16[192,1536]{1,0:T(8,128)(2,1)}, u32[]{:S(2)}) copy-start(bf16[192,1536]{1,0:T(8,128)(2,1)} %broadcast_select_fusion) | copy-start | bytes 1769476
  479.2 20.5 %collective-permute-start.8 = (bf16[192,1536]{1,0:T(8,128)(2,1)}, bf16[192,1536]{1,0:T(8,128)(2,1)S(1)}, u32[]{:S(2)}, u32[]{:S(2)}) collective-permute-start(bf16[192,1536]{1,0:T(8,128)(2,1)} %fusion.13), channel_id=1, source_target_pairs={{0,16},{8,24},{16,32},{24,40},{32,48},{40,56},{48,64},{56,72},{64,... | collective-permute-start | bytes 1769480 | tf_op jit(solution)/shard_map/ppermute | solution.py:10
  485.1 23.3 %collective-permute-start.7 = (bf16[192,1536]{1,0:T(8,128)(2,1)S(1)}, bf16[192,1536]{1,0:T(8,128)(2,1)S(1)}, u32[]{:S(2)}, u32[]{:S(2)}) collective-permute-start(bf16[192,1536]{1,0:T(8,128)(2,1)S(1)} %convolution_convert_fusion), channel_id=1, source_target_pairs={{0,16},{8,24},{16,32},{24,40},{32,48},{40,56},{48,64},{56,72},{64,... | collective-permute-start | bytes 1769480 | tf_op jit(solution)/shard_map/ppermute | solution.py:10
  487.5 6.9 %collective-permute-start.6 = (bf16[1536]{0:T(1024)(128)(2,1)S(1)}, bf16[1536]{0:T(1024)(128)(2,1)S(1)}, u32[]{:S(2)}, u32[]{:S(2)}) collective-permute-start(bf16[1536]{0:T(1024)(128)(2,1)S(1)} %all-reduce.1), channel_id=1, source_target_pairs={{16,0},{24,8},{32,16},{40,24},{48,32},{56,40},{64,48},{72,56},{80,... | collective-permute-start | bytes 9224 | tf_op jit(solution)/shard_map/ppermute | solution.py:10
Sparse Core Ops, SparseCore 0:
  10.4 106.8 all-gather.3
  122.3 58.3 all-gather.5
  289.7 56.8 all-gather.7
where the time goes:
time: 521 us; the launch traced here: 520 us
  waiting for transfers between devices  394 us (76%)
  matrix products  39.3 us (8%)
  starting transfers between devices  31.4 us (6%)
  blocking collectives  31 us (6%)
  between operations  14.6 us (3%)
  local copies, waits for them, and re-layouts  5.8 us (1%)
    ppermute x9, waiting for transfers between devices, passed_along(): return lax.ppermute(block, axis, route)  171 us
    all_gather x2, waiting for transfers between devices, reduce_level(): own_full = lax.all_gather(link, 'space', axis=0, tiled=True)  115 us
    all_gather x1, waiting for transfers between devices, on_device(): piece_rows = lax.all_gather(couple_pair, 'space', axis=1, tiled=True)  107 us
    ppermute x9, starting transfers between devices, passed_along(): return lax.ppermute(block, axis, route)  31.3 us
    unnamed x2, blocking collectives  31 us
    dot_general x5, matrix products, outer_form(): jnp.einsum('ik,jk->ij', left_side, right_side, preferred_element_type=jnp...  23.8 us
  transfers between devices with their start and end apart: 12, of which 9 were waited for; matrix products, arithmetic and copies ran while one was open for 5% of the time, Pallas kernels for 0%

commit v1 on v0

--- a/solution.py
+++ b/solution.py
@@ -60,7 +60,9 @@
     own_scaled = scaled_by(own_rows, reciprocal)
     prev_scaled = scaled_by(prev_rows, reciprocal)
     couple_pair = jnp.stack([own_rows, prev_rows])
-    piece_rows = lax.all_gather(couple_pair, "space", axis=1, tiled=True)
+    piece_rows = jnp.concatenate(
+        lax.all_to_all(jnp.stack([couple_pair] * lax.axis_size("space")), "space", 0, 0), axis=1
+    )
     local_forms = jnp.stack(
         [
             outer_form(own_scaled, piece_rows[0]),

time: 521 us -> 639 us (1.23)
  waiting for transfers between devices: 394 us -> 493 us
  local copies, waits for them, and re-layouts: 5.8 us -> 18.6 us
  starting transfers between devices: 31.4 us -> 40.2 us
    all_to_all x0 -> x1, waiting for transfers between devices: none -> 209 us  [on_device(): lax.all_to_all(jnp.stack([couple_pair] * lax.axis_size('space')), 'space'...]
    all_gather x1 -> x0, waiting for transfers between devices: 107 us -> none  [on_device(): piece_rows = lax.all_gather(couple_pair, 'space', axis=1, tiled=True)]
    all_to_all x0 -> x1, starting transfers between devices: none -> 8.6 us  [on_device(): lax.all_to_all(jnp.stack([couple_pair] * lax.axis_size('space')), 'space'...]
    slice x0 -> x1, local copies, waits for them, and re-layouts: none -> 6.56 us  [on_device(): piece_rows[0]]
  transfers between devices with their start and end apart: 12 -> 12, of which waited for: 9 -> 9; matrix products, arithmetic and copies ran while one was open for 5% -> 4% of each run, Pallas kernels for 0% -> 0%
where the time goes in v1:
time: 639 us; the launch traced here: 638 us
  waiting for transfers between devices  493 us (77%)
  starting transfers between devices  40.2 us (6%)
  matrix products  37.1 us (6%)
  blocking collectives  31 us (5%)
  local copies, waits for them, and re-layouts  18.6 us (3%)
  between operations  15 us (2%)
    all_to_all x1, waiting for transfers between devices, on_device(): lax.all_to_all(jnp.stack([couple_pair] * lax.axis_size('space')), 'space'...  209 us
    ppermute x9, waiting for transfers between devices, passed_along(): return lax.ppermute(block, axis, route)  171 us
    all_gather x2, waiting for transfers between devices, reduce_level(): own_full = lax.all_gather(link, 'space', axis=0, tiled=True)  113 us
    ppermute x9, starting transfers between devices, passed_along(): return lax.ppermute(block, axis, route)  31.5 us
    unnamed x2, blocking collectives  31 us
    dot_general x5, matrix products, outer_form(): jnp.einsum('ik,jk->ij', left_side, right_side, preferred_element_type=jnp...  21.6 us
  transfers between devices with their start and end apart: 12, of which 9 were waited for; matrix products, arithmetic and copies ran while one was open for 4% of the time, Pallas kernels for 0%

profile of v1, /device:TPU:6, one launch (start us, length us, event | category | flops | bytes accessed | tf_op | source)
XLA Modules:
  0.0 638.2 jit_solution(5741723622056131000)
XLA Ops:
  8.5 4.6 stack.5
  13.1 8.6 %all-to-all-start = ((bf16[8,2,192,1536]{3,2,1,0:T(8,128)(2,1)}), bf16[8,2,192,1536]{3,2,1,0:T(8,128)(2,1)}, u32[]{:S(2)}, u32[]{:S(2)}) async-start(bf16[8,2,192,1536]{3,2,1,0:T(8,128)(2,1)} %stack.5), calls=%async_computation | async-start | bytes 18874368 | tf_op jit(solution)/shard_map/all_to_all | solution.py:64
  21.8 209.1 %all-to-all-done = bf16[8,2,192,1536]{3,2,1,0:T(8,128)(2,1)} async-done(((bf16[8,2,192,1536]{3,2,1,0:T(8,128)(2,1)}), bf16[8,2,192,1536]{3,2,1,0:T(8,128)(2,1)}, u32[]{:S(2)}, u32[]{:S(2)}) %all-to-all-start) | async-done | bytes 9437216 | tf_op jit(solution)/shard_map/all_to_all | solution.py:64
  230.9 6.6 %fusion.33 = (bf16[1,8,192,1536]{3,2,0,1:T(8,128)(2,1)S(1)}, bf16[1,8,192,1536]{3,2,0,1:T(8,128)(2,1)}) fusion(bf16[2,8,192,1536]{3,2,0,1:T(8,128)(2,1)} %bitcast.2), kind=kLoop, calls=%fused_computation.57 | loop fusion | bytes 18874368 | tf_op jit(solution)/shard_map/slice | solution.py:68
  242.3 56.1 %all-gather.3.cloned.1.call-done = bf16[1536,1536]{1,0:T(8,128)(2,1)} async-done(((bf16[192,1536]{1,0:T(8,128)(2,1)}), bf16[1536,1536]{1,0:T(8,128)(2,1)}) %all-gather.3.cloned.1.call-update) | async-done | bytes 4718608 | tf_op jit(solution)/shard_map/all_gather | solution.py:26
  298.4 4.4 collective-permute-start.1
  302.8 5.2 fusion.25
  311.8 55.5 %collective-permute-done = f32[192,1536]{1,0:T(8,128)} collective-permute-done((f32[192,1536]{1,0:T(8,128)}, f32[192,1536]{1,0:T(8,128)}, u32[]{:S(2)}, u32[]{:S(2)}) %collective-permute-start) | collective-permute-done | bytes 1179680 | tf_op jit(solution)/shard_map/ppermute | solution.py:10
  367.3 4.4 fusion.5
  374.1 15.5 %all-reduce = bf16[1536]{0:T(1024)(128)(2,1)S(1)} all-reduce(bf16[1536]{0:T(1024)(128)(2,1)S(1)} %dynamic-update-slice), channel_id=1, replica_groups=mesh['tm'=32,'space'=8] {'space'}, use_global_device_ids=true, to_apply=%add | all-reduce | flops 1536 | bytes 6144
  395.0 11.4 %collective-permute-done.4 = bf16[192,1536]{1,0:T(8,128)(2,1)S(1)} collective-permute-done((bf16[192,1536]{1,0:T(8,128)(2,1)S(1)}, bf16[192,1536]{1,0:T(8,128)(2,1)S(1)}, u32[]{:S(2)}, u32[]{:S(2)}) %collective-permute-start.4) | collective-permute-done | bytes 589856 | tf_op jit(solution)/shard_map/ppermute | solution.py:10
  407.3 57.0 %all-gather.5.cloned.1.call-done = bf16[1536,1536]{1,0:T(8,128)(2,1)} async-done(((bf16[192,1536]{1,0:T(8,128)(2,1)}), bf16[1536,1536]{1,0:T(8,128)(2,1)}) %all-gather.5.cloned.1.call-update) | async-done | bytes 4718608 | tf_op jit(solution)/shard_map/all_gather | solution.py:26
  464.3 4.9 collective-permute-start.5
  469.2 3.9 convolution_convert_fusion.1
  475.1 5.8 collective-permute-start.2
  480.9 89.7 %collective-permute-done.2 = bf16[1536]{0:T(1024)(128)(2,1)S(1)} collective-permute-done((bf16[1536]{0:T(1024)(128)(2,1)S(1)}, bf16[1536]{0:T(1024)(128)(2,1)S(1)}, u32[]{:S(2)}, u32[]{:S(2)}) %collective-permute-start.2) | collective-permute-done | bytes 3104 | tf_op jit(solution)/shard_map/ppermute | solution.py:10
  570.6 4.2 fusion.4
  577.2 15.5 %all-reduce.1 = bf16[1536]{0:T(1024)(128)(2,1)S(1)} all-reduce(bf16[1536]{0:T(1024)(128)(2,1)S(1)} %dynamic-update-slice.1), channel_id=1, replica_groups=mesh['tm'=32,'space'=8] {'space'}, use_global_device_ids=true, to_apply=%add.1 | all-reduce | flops 1536 | bytes 6144
  592.7 4.3 fusion.8
  599.1 3.9 convolution_convert_fusion
  605.4 5.6 collective-permute-start.6
  612.3 5.1 collective-permute-done.8
  618.3 7.8 %collective-permute-done.7 = bf16[192,1536]{1,0:T(8,128)(2,1)S(1)} collective-permute-done((bf16[192,1536]{1,0:T(8,128)(2,1)S(1)}, bf16[192,1536]{1,0:T(8,128)(2,1)S(1)}, u32[]{:S(2)}, u32[]{:S(2)}) %collective-permute-start.7) | collective-permute-done | bytes 589856 | tf_op jit(solution)/shard_map/ppermute | solution.py:10
  626.1 5.2 fusion.2
  (51 shorter events, 28.8 us)
Async XLA Ops:
  13.1 8.7 %copy-start.6 = (f32[1,1536]{1,0:T(1,128)S(1)}, f32[1,1536]{1,0:T(1,128)}, u32[]{:S(2)}) copy-start(f32[1,1536]{1,0:T(1,128)} %param.7) | copy-start | bytes 18436
  13.1 217.8 %all-to-all-start = ((bf16[8,2,192,1536]{3,2,1,0:T(8,128)(2,1)}), bf16[8,2,192,1536]{3,2,1,0:T(8,128)(2,1)}, u32[]{:S(2)}, u32[]{:S(2)}) async-start(bf16[8,2,192,1536]{3,2,1,0:T(8,128)(2,1)} %stack.5), calls=%async_computation | async-start | bytes 18874368 | tf_op jit(solution)/shard_map/all_to_all | solution.py:64
  21.7 276.7 %all-gather.3.cloned.1.call-start = ((), (), s32[]{:S(2)}) async-start(), calls=%async_computation.1 | async-start | bytes 5308416 | tf_op jit(solution)/shard_map/all_gather | solution.py:26
  230.9 8.8 %copy-start.5 = (bf16[1,192,1536]{2,1,0:T(8,128)(2,1)S(1)}, bf16[1,192,1536]{2,1,0:T(8,128)(2,1)}, u32[]{:S(2)}) copy-start(bf16[1,192,1536]{2,1,0:T(8,128)(2,1)} %param.6) | copy-start | bytes 1769476
  237.4 2.2 copy-start
  242.2 222.1 %all-gather.5.cloned.1.call-start = ((), (), s32[]{:S(2)}) async-start(), calls=%async_computation.2 | async-start | bytes 5308416 | tf_op jit(solution)/shard_map/all_gather | solution.py:26
  298.4 91.2 %collective-permute-start.1 = (bf16[1536,1536]{1,0:T(8,128)(2,1)}, bf16[1536,1536]{1,0:T(8,128)(2,1)}, u32[]{:S(2)}, u32[]{:S(2)}) collective-permute-start(bf16[1536,1536]{1,0:T(8,128)(2,1)} %all-gather.3.cloned.1.call-done), channel_id=1, source_target_pairs={{8,0},{16,8},{24,16},{32,24},{40,32},{48,40},{56,48},{64,56},{72,6... | collective-permute-start | bytes 14155784 | tf_op jit(solution)/shard_map/ppermute | solution.py:10
  302.8 7.8 %copy-start.7 = (u32[256]{0:T(256)S(1)}, u32[256]{0:T(256)}, u32[]{:S(2)}) copy-start(u32[256]{0:T(256)} %constant.83) | copy-start | bytes 3076
  302.8 64.6 %copy-start.2 = (bf16[1,192,1536]{2,1,0:T(8,128)(2,1)S(1)}, bf16[1,192,1536]{2,1,0:T(8,128)(2,1)}, u32[]{:S(2)}) copy-start(bf16[1,192,1536]{2,1,0:T(8,128)(2,1)} %param.5) | copy-start | bytes 1769476
  302.8 64.6 %copy-start.4 = (f32[1,192,1536]{2,1,0:T(8,128)S(1)}, f32[1,192,1536]{2,1,0:T(8,128)}, u32[]{:S(2)}) copy-start(f32[1,192,1536]{2,1,0:T(8,128)} %param.4) | copy-start | bytes 3538948
  308.0 59.4 %collective-permute-start = (f32[192,1536]{1,0:T(8,128)}, f32[192,1536]{1,0:T(8,128)}, u32[]{:S(2)}, u32[]{:S(2)}) collective-permute-start(f32[192,1536]{1,0:T(8,128)} %fusion.25), channel_id=1, source_target_pairs={{8,0},{16,8},{24,16},{32,24},{40,32},{48,40},{56,48},{64,56},{72,6... | collective-permute-start | bytes 3538952 | tf_op jit(solution)/shard_map/ppermute | solution.py:10
  371.8 17.9 %copy-start.3 = (bf16[192,1536]{1,0:T(8,128)(2,1)S(1)}, bf16[192,1536]{1,0:T(8,128)(2,1)}, u32[]{:S(2)}) copy-start(bf16[192,1536]{1,0:T(8,128)(2,1)} %fusion.9) | copy-start | bytes 1769476
  393.1 13.3 %collective-permute-start.4 = (bf16[192,1536]{1,0:T(8,128)(2,1)S(1)}, bf16[192,1536]{1,0:T(8,128)(2,1)S(1)}, u32[]{:S(2)}, u32[]{:S(2)}) collective-permute-start(bf16[192,1536]{1,0:T(8,128)(2,1)S(1)} %fusion.7), channel_id=1, source_target_pairs={{0,8},{8,16},{16,24},{24,32},{32,40},{40,48},{48,56},{56,64},{64,7... | collective-permute-start | bytes 1769480 | tf_op jit(solution)/shard_map/ppermute | solution.py:10
  464.3 128.4 %collective-permute-start.5 = (bf16[1536,1536]{1,0:T(8,128)(2,1)}, bf16[1536,1536]{1,0:T(8,128)(2,1)}, u32[]{:S(2)}, u32[]{:S(2)}) collective-permute-start(bf16[1536,1536]{1,0:T(8,128)(2,1)} %all-gather.5.cloned.1.call-done), channel_id=1, source_target_pairs={{16,0},{24,8},{32,16},{40,24},{48,32},{56,40},{64,48},{72,56},{80,... | collective-permute-start | bytes 14155784 | tf_op jit(solution)/shard_map/ppermute | solution.py:10
  473.2 97.4 %collective-permute-start.3 = (bf16[192,1536]{1,0:T(8,128)(2,1)S(1)}, bf16[192,1536]{1,0:T(8,128)(2,1)S(1)}, u32[]{:S(2)}, u32[]{:S(2)}) collective-permute-start(bf16[192,1536]{1,0:T(8,128)(2,1)S(1)} %convolution_convert_fusion.1), channel_id=1, source_target_pairs={{0,8},{8,16},{16,24},{24,32},{32,40},{40,48},{48,56},{56,64},{64,7... | collective-permute-start | bytes 1769480 | tf_op jit(solution)/shard_map/ppermute | solution.py:10
  475.1 95.5 %collective-permute-start.2 = (bf16[1536]{0:T(1024)(128)(2,1)S(1)}, bf16[1536]{0:T(1024)(128)(2,1)S(1)}, u32[]{:S(2)}, u32[]{:S(2)}) collective-permute-start(bf16[1536]{0:T(1024)(128)(2,1)S(1)} %all-reduce), channel_id=1, source_target_pairs={{8,0},{16,8},{24,16},{32,24},{40,32},{48,40},{56,48},{64,56},{72,6... | collective-permute-start | bytes 9224 | tf_op jit(solution)/shard_map/ppermute | solution.py:10
  574.8 17.9 %copy-start.1 = (bf16[192,1536]{1,0:T(8,128)(2,1)S(1)}, bf16[192,1536]{1,0:T(8,128)(2,1)}, u32[]{:S(2)}) copy-start(bf16[192,1536]{1,0:T(8,128)(2,1)} %broadcast_select_fusion) | copy-start | bytes 1769476
  597.0 20.5 %collective-permute-start.8 = (bf16[192,1536]{1,0:T(8,128)(2,1)}, bf16[192,1536]{1,0:T(8,128)(2,1)S(1)}, u32[]{:S(2)}, u32[]{:S(2)}) collective-permute-start(bf16[192,1536]{1,0:T(8,128)(2,1)} %fusion.8), channel_id=1, source_target_pairs={{0,16},{8,24},{16,32},{24,40},{32,48},{40,56},{48,64},{56,72},{64,... | collective-permute-start | bytes 1769480 | tf_op jit(solution)/shard_map/ppermute | solution.py:10
  603.0 23.1 %collective-permute-start.7 = (bf16[192,1536]{1,0:T(8,128)(2,1)S(1)}, bf16[192,1536]{1,0:T(8,128)(2,1)S(1)}, u32[]{:S(2)}, u32[]{:S(2)}) collective-permute-start(bf16[192,1536]{1,0:T(8,128)(2,1)S(1)} %convolution_convert_fusion), channel_id=1, source_target_pairs={{0,16},{8,24},{16,32},{24,40},{32,48},{40,56},{48,64},{56,72},{64,... | collective-permute-start | bytes 1769480 | tf_op jit(solution)/shard_map/ppermute | solution.py:10
  605.4 6.9 %collective-permute-start.6 = (bf16[1536]{0:T(1024)(128)(2,1)S(1)}, bf16[1536]{0:T(1024)(128)(2,1)S(1)}, u32[]{:S(2)}, u32[]{:S(2)}) collective-permute-start(bf16[1536]{0:T(1024)(128)(2,1)S(1)} %all-reduce.1), channel_id=1, source_target_pairs={{16,0},{24,8},{32,16},{40,24},{48,32},{56,40},{64,48},{72,56},{80,... | collective-permute-start | bytes 9224 | tf_op jit(solution)/shard_map/ppermute | solution.py:10
Sparse Core Ops, SparseCore 0:
  242.3 56.0 all-gather.2
  407.4 56.8 all-gather.4
